TPU v7x, 512 devices: a whole 4x4x16 slice. The times are simulated.
512 devices in a mesh: alt: 8 (over x, y_hi), strip: 64 (over z, y_lo, core).
Axes of the slice: x: 4, y: 4 (y_hi: 2, y_lo: 2; y = y_hi * 2 + y_lo), z: 16, core: 2. Of those that a mesh axis runs over, the one named last changes fastest.
Arguments:
- screens: bfloat16 [16, 512, 512], P('alt', 'strip'), may hold values from -2.390625 to 2.390625
- row_offset: int32 [2, 16, 2], replicated, may hold values from 0 to 341, as said below
- col_offset: int32 [2, 16, 2], replicated, may hold values from 0 to 341, as said below
- layer_bin: int32 [16], replicated, may hold values from 0 to 15
- illumination: float32 [16, 12800], P(None, ('alt', 'strip')), may hold values from 0.3 to 1
- reconstructor: bfloat16 [2, 12800, 6000], P(None, ('alt', 'strip')), may hold values from -0.0390625 to 0.0390625
- sat_code: int32 [6000], replicated, may hold values from 1 to 16
Outputs:
- slopes: float32 [2, 2, 12800], P(None, None, ('alt', 'strip'))
- commands: float32 [2, 6000], replicated
Inputs may be any that keep to these rules, and one draw needn't show every extreme that they name: Every footprint lies inside the screen: row_offset[f, l, g] + (319) shrink_l <= 511. Every footprint lies inside the screen: col_offset[f, l, g] + (319) shrink_l <= 511.
All inputs are finite; a program needn't handle non-finite values.
Results may differ from a plain program's by a relative error of at most 0.0028.
Values sent between devices are 32-bit elements; how exact they have to be, the bound alone decides.
No kernel may reach another device: no remote copies, remote signals or barrier semaphores. Data moves between devices by JAX's collectives and lax.ppermute only.
A program may use at most 64 MiB of HBM per device.

v0:
```python
import math
import jax
import jax.numpy as jnp
from jax import lax
from jax.sharding import PartitionSpec as P

LENSLETS = 80
PIXELS = 4
GUIDE_STARS = 2
FRAMES = 2
ACTUATORS = 6000
PUPIL_PIX = 320
WINDOW = 384
SUBAPS_ALL = 12800
highest = lax.Precision.HIGHEST
loop_gain = 0.5
code_step = 0.125
bin_step = 0.03125


def bilinear(offsets):
    return jnp.maximum(0.0, 1.0 - jnp.abs(offsets))


def dft_tables():
    padded = 2 * PIXELS
    freq_index = jnp.arange(padded * padded, dtype=jnp.int32)
    freq_row = freq_index // padded
    freq_col = freq_index % padded
    pix_index = jnp.arange(PIXELS * PIXELS, dtype=jnp.int32)
    pix_row = pix_index // PIXELS
    pix_col = pix_index % PIXELS
    turn_count = (
        freq_row[:, None] * pix_row[None, :] + freq_col[:, None] * pix_col[None, :]
    ) % padded
    angles = turn_count.astype(jnp.float32) * (2.0 * math.pi / padded)
    coord_row = ((freq_row + PIXELS) % padded - PIXELS).astype(jnp.float32)
    coord_col = ((freq_col + PIXELS) % padded - PIXELS).astype(jnp.float32)
    return (jnp.cos(angles), jnp.sin(angles), coord_row, coord_col)


def centroids(pupil_phase, illumination, tables):
    cosine, sine_table, coord_row, coord_col = tables
    field_re = illumination * jnp.cos(pupil_phase)
    field_im = illumination * jnp.sin(pupil_phase)
    real_part = jnp.dot(cosine, field_re, precision=highest) + jnp.dot(
        sine_table, field_im, precision=highest
    )
    imag_part = jnp.dot(cosine, field_im, precision=highest) - jnp.dot(
        sine_table, field_re, precision=highest
    )
    intensity = real_part * real_part + imag_part * imag_part
    flux_sum = jnp.sum(intensity, axis=0)
    slope_row = jnp.sum(intensity * coord_row[:, None], axis=0) / flux_sum
    slope_col = jnp.sum(intensity * coord_col[:, None], axis=0) / flux_sum
    return jnp.stack([slope_row, slope_col])


def shards(screens, row_offset, col_offset, layer_bin, illumination, reconstructor, sat_code):
    layer_dev = screens.shape[0]
    rows_here = screens.shape[1]
    count_here = illumination.shape[1]
    group_pos = lax.axis_index("alt")
    strip_pos = lax.axis_index("strip")
    row_global = strip_pos * rows_here + jnp.arange(rows_here, dtype=jnp.int32)
    pupil_idx = jnp.arange(PUPIL_PIX, dtype=jnp.float32)
    window_idx = jnp.arange(WINDOW, dtype=jnp.float32)
    widened_layers = [
        jnp.pad(screens[layer_no], ((0, 0), (0, WINDOW))) for layer_no in range(layer_dev)
    ]
    frame_terms = []
    for frame_no in range(FRAMES):
        running = jnp.zeros((PIXELS, PIXELS, GUIDE_STARS, LENSLETS, LENSLETS), jnp.float32)
        for layer_no in range(layer_dev):
            layer_pos = group_pos * layer_dev + layer_no
            tops = lax.dynamic_index_in_dim(row_offset[frame_no], layer_pos, 0, keepdims=False)
            lefts = lax.dynamic_index_in_dim(col_offset[frame_no], layer_pos, 0, keepdims=False)
            bin_value = lax.dynamic_index_in_dim(layer_bin, layer_pos, 0, keepdims=False)
            shrink = 1.0 - bin_value.astype(jnp.float32) * bin_step
            col_weights = bilinear(window_idx[None, :] - pupil_idx[:, None] * shrink)
            widened = widened_layers[layer_no]

            def cut_columns(left_col):
                return lax.dynamic_slice_in_dim(widened, left_col, WINDOW, 1)

            strips = jax.vmap(cut_columns)(lefts).astype(jnp.float32)
            across = jnp.einsum("drc,jc->drj", strips, col_weights, precision=highest)
            offsets = (row_global[None, :] - tops[:, None]).astype(jnp.float32)
            row_weights = bilinear(offsets[:, None, :] - pupil_idx[None, :, None] * shrink)
            running = running + jnp.einsum(
                "dapr,drbq->pqdab",
                row_weights.reshape(GUIDE_STARS, LENSLETS, PIXELS, rows_here),
                across.reshape(GUIDE_STARS, rows_here, LENSLETS, PIXELS),
                precision=highest,
            )
        frame_terms.append(running.reshape(PIXELS * PIXELS, SUBAPS_ALL))
    phase_terms = jnp.concatenate(frame_terms, axis=0)
    owned = lax.psum_scatter(phase_terms, ("alt", "strip"), scatter_dimension=1, tiled=True)
    pupil_phase = owned.reshape(FRAMES, PIXELS * PIXELS, count_here)
    tables = dft_tables()
    slopes = jnp.stack(
        [centroids(pupil_phase[frame_no], illumination, tables) for frame_no in range(FRAMES)]
    )
    rounded = slopes.astype(jnp.bfloat16).reshape(FRAMES, 2 * count_here)
    partial_value = jnp.dot(
        rounded,
        reconstructor.reshape(2 * count_here, ACTUATORS),
        preferred_element_type=jnp.float32,
    )
    updates = lax.psum(partial_value, ("alt", "strip"))
    limits = sat_code.astype(jnp.float32) * code_step
    first_cmd = jnp.clip(loop_gain * updates[0], -limits, limits)
    second_cmd = jnp.clip(first_cmd + loop_gain * updates[1], -limits, limits)
    return (slopes, jnp.stack([first_cmd, second_cmd]))


def solution(mesh):
    placed = (
        P("alt", "strip", None),
        P(),
        P(),
        P(),
        P(None, ("alt", "strip")),
        P(None, ("alt", "strip"), None),
        P(),
    )
    return jax.shard_map(
        shards,
        mesh=mesh,
        in_specs=placed,
        out_specs=(P(None, None, ("alt", "strip")), P()),
        check_vma=False,
    )
```

profile of v0, /device:TPU:1, one launch (start us, length us, event | category | flops | bytes accessed | tf_op | source)
XLA Modules:
  0.0 635.3 jit_solution(2373824298019678638)
XLA Ops:
  7.2 1.4 fusion.161
  12.6 2.7 while.4
  15.5 2.5 while.5
  19.2 1.2 fusion.21
  20.5 1.2 fusion.1
  22.1 1.7 reshape.445
  24.2 2.7 while.6
  27.6 2.6 while.7
  28.2 0.7 bitcast_dynamic-update-slice_fusion.11
  29.5 0.7 bitcast_dynamic-update-slice_fusion.11
  30.8 1.2 fusion.18
  32.0 1.2 fusion
  33.7 1.7 reshape.448
  35.4 2.5 pad_maximum_fusion
  38.0 477.4 %all-reduce.9.cloned.1.call-done = f32[32,12800]{1,0:T(8,128)} async-done(((f32[32,12800]{1,0:T(8,128)}), f32[32,12800]{1,0:T(8,128)}) %all-reduce.9.cloned.1.call-update) | async-done | bytes 1638416
  515.4 1.1 fusion.84
  516.5 1.1 fusion.82
  517.6 1.1 fusion.80
  518.7 1.1 fusion.78
  519.9 1.1 fusion.4
  521.0 1.1 fusion.7
  522.2 1.1 fusion.6
  523.3 1.3 multiply_reduce_fusion.1
  525.0 102.0 %psum.7 = f32[2,6000]{1,0:T(2,128)S(1)} all-reduce(f32[2,6000]{1,0:T(2,128)S(1)} %convolution_bitcast_fusion), channel_id=1, replica_groups=mesh['alt'=8,'strip'=64] {'alt','strip'}, use_global_device_ids=true, to_apply=%region_7.8 | all-reduce | flops 12000 | bytes 96000 | tf_op jit(solution)/shard_map/psum | solution.py:110
  (81 shorter events, 17.3 us)
Async XLA Ops:
  7.2 517.5 %copy-start = (bf16[2,25,6000]{2,0,1:T(2,128)(2,1)S(1)}, bf16[2,25,6000]{2,0,1:T(2,128)(2,1)}, u32[]{:S(2)}) copy-start(bf16[2,25,6000]{2,0,1:T(2,128)(2,1)} %param.12) | copy-start | bytes 1800004
  7.2 508.2 %all-reduce.9.cloned.1.call-start = ((), (), s32[]{:S(2)}) async-start(), calls=%async_computation | async-start | bytes 3276800
  33.6 1.7 copy-start.1
  37.9 477.5 %copy-start.3 = (f32[16,25]{1,0:T(8,128)S(1)}, f32[16,25]{1,0:T(8,128)}, u32[]{:S(2)}) copy-start(f32[16,25]{1,0:T(8,128)} %param.11) | copy-start | bytes 4804
  37.9 589.2 %copy-start.2 = (s32[6000]{0:T(1024)S(1)}, s32[6000]{0:T(1024)}, u32[]{:S(2)}) copy-start(s32[6000]{0:T(1024)} %param.13) | copy-start | bytes 72004
Sparse Core Ops, SparseCore 0:
  38.0 477.3 all-reduce.8
where the time goes:
time: 636 us; the launch traced here: 635 us
  waiting for transfers between devices  477 us (75%)
  blocking collectives  102 us (16%)
  local copies, waits for them, and re-layouts  20.2 us (3%)
  matrix products  16.4 us (3%)
  between operations  15.7 us (2%)
    unnamed x2, waiting for transfers between devices  477 us
    psum x1, blocking collectives, shards(): updates = lax.psum(partial_value, ('alt', 'strip'))  102 us
  transfers between devices with their start and end apart: 1, of which 1 were waited for; matrix products, arithmetic and copies ran while one was open for 0% of the time, Pallas kernels for 0%

commit v1 on v0

--- a/solution.py
+++ b/solution.py
@@ -107,7 +107,11 @@
         reconstructor.reshape(2 * count_here, ACTUATORS),
         preferred_element_type=jnp.float32,
     )
-    updates = lax.psum(partial_value, ("alt", "strip"))
+
+    def wait_map(t0):
+        return jax.lax.all_gather(t0, ("alt", "strip")).sum(axis=0)
+
+    updates = wait_map(partial_value)
     limits = sat_code.astype(jnp.float32) * code_step
     first_cmd = jnp.clip(loop_gain * updates[0], -limits, limits)
     second_cmd = jnp.clip(first_cmd + loop_gain * updates[1], -limits, limits)

time: 636 us -> 1390 us (2.19)
  waiting for transfers between devices: 477 us -> 1320 us
  blocking collectives: 102 us -> 0 us
    all_gather x0 -> x1, waiting for transfers between devices: none -> 838 us  [wait_map(): return jax.lax.all_gather(t0, ('alt', 'strip')).sum(axis=0)]
    psum x1 -> x0, blocking collectives: 102 us -> none  [shards(): updates = lax.psum(partial_value, ('alt', 'strip'))]
    unnamed x2 -> x3, waiting for transfers between devices: 477 us -> 477 us
  transfers between devices with their start and end apart: 1 -> 2, of which waited for: 1 -> 2; matrix products, arithmetic and copies ran while one was open for 0% -> 0% of each run, Pallas kernels for 0% -> 0%
where the time goes in v1:
time: 1390 us; the launch traced here: 1380 us
  waiting for transfers between devices  1320 us (95%)
  local copies, waits for them, and re-layouts  20.3 us (1%)
  matrix products  17.8 us (1%)
  between operations  15.7 us (1%)
    all_gather x1, waiting for transfers between devices, wait_map(): return jax.lax.all_gather(t0, ('alt', 'strip')).sum(axis=0)  838 us
    unnamed x3, waiting for transfers between devices  477 us
  transfers between devices with their start and end apart: 2, of which 2 were waited for; matrix products, arithmetic and copies ran while one was open for 0% of the time, Pallas kernels for 0%

profile of v1, /device:TPU:1, one launch (start us, length us, event | category | flops | bytes accessed | tf_op | source)
XLA Modules:
  0.0 1383.1 jit_solution(18230725256749544686)
XLA Ops:
  7.2 1.4 fusion.161
  13.3 2.8 while.7
  16.0 2.7 while.5
  18.7 2.5 while.6
  21.2 2.6 while.4
  23.9 1.2 fusion.15
  27.5 1.2 fusion.18
  28.7 1.2 fusion
  30.4 1.7 reshape.448
  32.1 1.2 fusion.21
  33.4 1.2 fusion.1
  35.0 1.7 reshape.445
  36.8 2.5 pad_maximum_fusion
  39.6 477.1 %all-reduce.9.cloned.1.call-done = f32[32,12800]{1,0:T(8,128)} async-done(((f32[32,12800]{1,0:T(8,128)}), f32[32,12800]{1,0:T(8,128)}) %all-reduce.9.cloned.1.call-update) | async-done | bytes 1638416
  516.7 1.1 fusion.82
  517.8 1.1 fusion.84
  518.9 1.1 fusion.78
  520.1 1.1 fusion.80
  521.2 1.1 fusion.7
  522.3 1.1 fusion.4
  523.5 1.1 fusion.6
  524.6 1.3 multiply_reduce_fusion.1
  527.6 838.5 %all-gather.4.cloned.1.call-done = f32[512,2,6000]{2,1,0:T(2,128)} async-done(((f32[1,2,6000]{2,1,0:T(2,128)}), f32[512,2,6000]{2,1,0:T(2,128)}) %all-gather.4.cloned.1.call-update) | async-done | bytes 24576016 | tf_op jit(solution)/shard_map/all_gather | solution.py:112
  1366.1 9.3 reduce_sum.69
  (94 shorter events, 19.8 us)
Async XLA Ops:
  7.2 518.9 %copy-start = (bf16[2,25,6000]{2,0,1:T(2,128)(2,1)S(1)}, bf16[2,25,6000]{2,0,1:T(2,128)(2,1)}, u32[]{:S(2)}) copy-start(bf16[2,25,6000]{2,0,1:T(2,128)(2,1)} %param.12) | copy-start | bytes 1800004
  7.2 509.5 %all-reduce.9.cloned.1.call-start = ((), (), s32[]{:S(2)}) async-start(), calls=%async_computation.1 | async-start | bytes 3276800
  10.0 17.6 %copy-start.4 = (f32[80,4]{0,1:T(4,128)}, f32[80,4]{0,1:T(4,128)S(1)}, u32[]{:S(2)}) copy-start(f32[80,4]{0,1:T(4,128)S(1)} %fusion.91) | copy-start | bytes 3844
  30.4 1.7 copy-start.2
  30.4 1.7 copy-start.5
  30.4 1.7 copy-start.7
  32.1 1.2 copy-start.6
  35.0 1.7 copy-start.1
  39.3 477.4 %copy-start.8 = (f32[16,25]{1,0:T(8,128)S(1)}, f32[16,25]{1,0:T(8,128)}, u32[]{:S(2)}) copy-start(f32[16,25]{1,0:T(8,128)} %param.11) | copy-start | bytes 4804
  39.3 1326.7 %all-gather.4.cloned.1.call-start = ((), (), s32[]{:S(2)}) async-start(), calls=%async_computation | async-start | bytes 24689664 | tf_op jit(solution)/shard_map/all_gather | solution.py:112
  527.6 847.9 %copy-start.3 = (s32[6000]{0:T(1024)S(1)}, s32[6000]{0:T(1024)}, u32[]{:S(2)}) copy-start(s32[6000]{0:T(1024)} %param.13) | copy-start | bytes 72004
Sparse Core Ops, SparseCore 0:
  39.5 477.2 all-reduce.8
  527.1 838.9 all-gather.3

commit v2 on v0

--- a/solution.py
+++ b/solution.py
@@ -107,7 +107,7 @@
         reconstructor.reshape(2 * count_here, ACTUATORS),
         preferred_element_type=jnp.float32,
     )
-    updates = lax.psum(partial_value, ("alt", "strip"))
+    updates = jax.lax.psum(jax.lax.psum(partial_value, "alt"), "strip")
     limits = sat_code.astype(jnp.float32) * code_step
     first_cmd = jnp.clip(loop_gain * updates[0], -limits, limits)
     second_cmd = jnp.clip(first_cmd + loop_gain * updates[1], -limits, limits)

time: 636 us -> 779 us (1.22)
  blocking collectives: 102 us -> 244 us
    psum x1 -> x2, blocking collectives: 102 us -> 244 us  [shards(): updates = jax.lax.psum(jax.lax.psum(partial_value, 'alt'), 'strip')]
where the time goes in v2:
time: 779 us; the launch traced here: 778 us
  waiting for transfers between devices  477 us (61%)
  blocking collectives  244 us (31%)
  local copies, waits for them, and re-layouts  20.2 us (3%)
  matrix products  16.4 us (2%)
  between operations  15.7 us (2%)
    unnamed x2, waiting for transfers between devices  477 us
    psum x2, blocking collectives, shards(): updates = jax.lax.psum(jax.lax.psum(partial_value, 'alt'), 'strip')  244 us
  transfers between devices with their start and end apart: 1, of which 1 were waited for; matrix products, arithmetic and copies ran while one was open for 0% of the time, Pallas kernels for 0%

profile of v2, /device:TPU:1, one launch (start us, length us, event | category | flops | bytes accessed | tf_op | source)
XLA Modules:
  0.0 777.6 jit_solution(12831771296193518723)
XLA Ops:
  7.2 1.4 fusion.161
  12.6 2.7 while.4
  15.5 2.5 while.5
  19.2 1.2 fusion.21
  20.5 1.2 fusion.1
  22.1 1.7 reshape.445
  24.2 2.7 while.6
  27.6 2.6 while.7
  29.5 0.7 bitcast_dynamic-update-slice_fusion.11
  30.8 1.2 fusion.18
  32.0 1.2 fusion
  33.7 1.7 reshape.448
  35.4 2.5 pad_maximum_fusion
  38.0 477.4 %all-reduce.9.cloned.1.call-done = f32[32,12800]{1,0:T(8,128)} async-done(((f32[32,12800]{1,0:T(8,128)}), f32[32,12800]{1,0:T(8,128)}) %all-reduce.9.cloned.1.call-update) | async-done | bytes 1638416
  515.4 1.1 fusion.84
  516.5 1.1 fusion.82
  517.6 1.1 fusion.80
  518.7 1.1 fusion.78
  519.9 1.1 fusion.4
  521.0 1.1 fusion.7
  522.2 1.1 fusion.6
  523.3 1.3 multiply_reduce_fusion.1
  525.0 34.9 %psum.14 = f32[2,6000]{1,0:T(2,128)S(1)} all-reduce(f32[2,6000]{1,0:T(2,128)S(1)} %convolution_bitcast_fusion), channel_id=1, replica_groups=mesh['alt'=8,'strip'=64] {'alt'}, use_global_device_ids=true, to_apply=%region_7.8 | all-reduce | flops 12000 | bytes 96000 | tf_op jit(solution)/shard_map/psum | solution.py:110
  559.9 209.5 %psum.15 = f32[2,6000]{1,0:T(2,128)S(1)} all-reduce(f32[2,6000]{1,0:T(2,128)S(1)} %psum.14), channel_id=1, replica_groups=mesh['alt'=8,'strip'=64] {'strip'}, use_global_device_ids=true, to_apply=%region_8.9 | all-reduce | flops 12000 | bytes 96000 | tf_op jit(solution)/shard_map/psum | solution.py:110
  (82 shorter events, 18.0 us)
Async XLA Ops:
  7.2 517.5 %copy-start = (bf16[2,25,6000]{2,0,1:T(2,128)(2,1)S(1)}, bf16[2,25,6000]{2,0,1:T(2,128)(2,1)}, u32[]{:S(2)}) copy-start(bf16[2,25,6000]{2,0,1:T(2,128)(2,1)} %param.12) | copy-start | bytes 1800004
  7.2 508.2 %all-reduce.9.cloned.1.call-start = ((), (), s32[]{:S(2)}) async-start(), calls=%async_computation | async-start | bytes 3276800
  33.6 1.7 copy-start.1
  37.9 477.5 %copy-start.3 = (f32[16,25]{1,0:T(8,128)S(1)}, f32[16,25]{1,0:T(8,128)}, u32[]{:S(2)}) copy-start(f32[16,25]{1,0:T(8,128)} %param.11) | copy-start | bytes 4804
  37.9 731.6 %copy-start.2 = (s32[6000]{0:T(1024)S(1)}, s32[6000]{0:T(1024)}, u32[]{:S(2)}) copy-start(s32[6000]{0:T(1024)} %param.13) | copy-start | bytes 72004
Sparse Core Ops, SparseCore 0:
  38.0 477.3 all-reduce.8
